TPU v7x, 256 devices: a whole 4x4x8 slice. The times are simulated.
256 devices in a mesh: pipe: 4 (over y), tensor: 32 (over z, x), dp: 2 (over core).
Axes of the slice: x: 4, y: 4, z: 8, core: 2. Of those that a mesh axis runs over, the one named last changes fastest.
Arguments:
- states: bfloat16 [4, 2, 128, 4096], P('pipe', 'dp', 'tensor'), may hold values from -6 to 6
- out_grad: bfloat16 [2, 128, 4096], P('dp', 'tensor'), may hold values from -6 to 6
- norm_gain: bfloat16 [4, 4096], P('pipe'), may hold values from 0.5 to 1.5
- gate_tiles: bfloat16 [4, 3520, 128, 128], P('pipe', 'tensor'), may hold values from -0.125 to 0.125
- up_tiles: bfloat16 [4, 3520, 128, 128], P('pipe', 'tensor'), may hold values from -0.125 to 0.125
- down_tiles: bfloat16 [4, 3520, 128, 128], P('pipe', 'tensor'), may hold values from -0.0625 to 0.0625
- tile_lists: int32 [4, 3, 3520, 2], P('pipe', None, 'tensor'), may hold values from 0 to 31, as said below
- tile_counts: int32 [4, 3, 32], P('pipe', None, 'tensor'), may hold values from 50 to 110, as said below
- gate_a: bfloat16 [4, 4096, 64], P('pipe'), may hold values from -0.09375 to 0.09375
- gate_adapter_output: bfloat16 [4, 64, 20480], P('pipe', None, 'tensor'), may hold values from -0.75 to 0.75
- up_a: bfloat16 [4, 4096, 64], P('pipe'), may hold values from -0.09375 to 0.09375
- upper_adapter_output: bfloat16 [4, 64, 20480], P('pipe', None, 'tensor'), may hold values from -0.75 to 0.75
- down_adapter_input: bfloat16 [4, 20480, 64], P('pipe', 'tensor'), may hold values from -0.0390625 to 0.0390625
- down_b: bfloat16 [4, 64, 4096], P('pipe'), may hold values from -0.75 to 0.75
Outputs:
- section_grads: bfloat16 [4, 2, 128, 4096], P('pipe', 'dp', 'tensor')
- grad_gate_a: bfloat16 [4, 4096, 64], P('pipe')
- grad_gate_b: bfloat16 [4, 64, 20480], P('pipe', None, 'tensor')
- grad_up_a: bfloat16 [4, 4096, 64], P('pipe')
- grad_up_b: bfloat16 [4, 64, 20480], P('pipe', None, 'tensor')
- grad_down_a: bfloat16 [4, 20480, 64], P('pipe', 'tensor')
- grad_down_b: bfloat16 [4, 64, 4096], P('pipe')
Inputs may be any that keep to these rules, and one draw needn't show every extreme that they name: `tile_counts`: entry [s, p, j] counts the kept tiles of shard j of projection p at section s; shard j and the shard half the tensor axis away keep exactly 160 tiles together. `tile_lists`: entries [s, p, j * 110 + k] give (row block, column block) of stored tile k of shard j, within the shard's own blocks; for gate and up the rows run over the 4096 features, for down over the shard's hidden units. The first counted entries of a shard name distinct blocks; the rest are unused.
All inputs are finite; a program needn't handle non-finite values.
Results may differ from a plain program's by a relative error of at most 0.035.
Values may be sent and summed in bfloat16 or wider, within the bound.
A program may use at most 192 MiB of HBM per device.

v0:
```python
import jax
import jax.numpy as jnp
from jax import lax
from jax.sharding import PartitionSpec as P

EPSILON = 1e-05
ADAPTER_SCALE = 0.25
EXACT_PRECISION = lax.Precision.HIGHEST


def passed_along(block, axis, distance):
    devices = range(lax.axis_size(axis))
    route = [(i - distance, i) for i in devices if i - distance in devices]
    return lax.ppermute(block, axis, route)


def exact_product(left, right):
    return jnp.dot(left.astype(jnp.float32), right.astype(jnp.float32), precision=EXACT_PRECISION)


def tile_product(operand, stacked, source, target, active, out_blocks, forward):
    picked = jnp.take(operand, source, axis=1).astype(jnp.float32)
    stacked_wide = stacked.astype(jnp.float32)
    if forward:
        product = jnp.einsum("tki,kij->ktj", picked, stacked_wide, precision=EXACT_PRECISION)
    else:
        product = jnp.einsum("tkj,kij->kti", picked, stacked_wide, precision=EXACT_PRECISION)
    slots = product.shape[0]
    routing = jnp.logical_and(
        target[None, :] == jnp.arange(out_blocks)[:, None], active[None, :]
    ).astype(jnp.float32)
    routed = jnp.dot(routing, product.reshape(slots, -1), precision=EXACT_PRECISION)
    return routed.reshape(out_blocks, operand.shape[0], -1).transpose(1, 0, 2)


def silu_parts(gate_activation):
    sigmoid = jax.nn.sigmoid(gate_activation)
    return (gate_activation * sigmoid, sigmoid * (1.0 + gate_activation * (1.0 - sigmoid)))


def shards(
    states,
    out_grad,
    norm_gain,
    gate_tiles,
    up_tiles,
    down_tiles,
    tile_lists,
    tile_counts,
    gate_a,
    gate_adapter_output,
    up_a,
    upper_adapter_output,
    down_adapter_input,
    down_b,
):
    pipe_size = lax.axis_size("pipe")
    tensor_size = lax.axis_size("tensor")
    section_now = lax.axis_index("pipe")
    model_width = states.shape[3]
    tile_size = gate_tiles.shape[-1]
    slot_count = gate_tiles.shape[1]
    rank_size = gate_a.shape[2]
    ff_shard = gate_adapter_output.shape[2]
    row_blocks = model_width // tile_size
    col_blocks = ff_shard // tile_size
    batch_count = states.shape[1]
    shard_rows = states.shape[2]
    piece_count = 1
    fold_count = 1
    piece_rows = shard_rows // piece_count
    row_count = piece_rows * tensor_size
    gain_row = norm_gain[0].astype(jnp.float32)
    stacks = (gate_tiles[0], up_tiles[0], down_tiles[0])
    positions = tile_lists[0]
    kept_counts = tile_counts[0, :, 0]
    tile_plans = []
    slot_ids = jnp.arange(slot_count)
    for member in range(3):
        tile_plans.append(
            (
                stacks[member],
                positions[member, :, 0],
                positions[member, :, 1],
                slot_ids < kept_counts[member],
                jnp.zeros((slot_count,), jnp.int32),
            )
        )

    def front(normed_all, grad_all):
        left_in = normed_all.reshape(row_count, row_blocks, tile_size)
        left_grad = grad_all.reshape(row_count, row_blocks, tile_size)
        outputs = []
        for member in range(2):
            held_tiles, rows_at, cols_at, active, partner = tile_plans[member]
            outputs.append(
                tile_product(
                    left_in, held_tiles, rows_at, cols_at, active, col_blocks * fold_count, True
                )
            )
        held_tiles, rows_at, cols_at, active, partner = tile_plans[2]
        outputs.append(
            tile_product(
                left_grad, held_tiles, cols_at, rows_at, active, col_blocks * fold_count, False
            )
        )
        return (outputs[0], outputs[1], outputs[2])

    def middle(normed_all, grad_all, gate_matmul, upper_matmul, hidden_matmul):
        gate_lowrank = exact_product(normed_all, gate_a[0]).astype(jnp.bfloat16)
        upper_lowrank = exact_product(normed_all, up_a[0]).astype(jnp.bfloat16)
        gradient_lowrank = exact_product(grad_all, down_b[0].T).astype(jnp.bfloat16)
        gate_activation = gate_matmul + ADAPTER_SCALE * exact_product(
            gate_lowrank, gate_adapter_output[0]
        )
        upward_projection = upper_matmul + ADAPTER_SCALE * exact_product(
            upper_lowrank, upper_adapter_output[0]
        )
        hidden_gradient = hidden_matmul + ADAPTER_SCALE * exact_product(
            gradient_lowrank, down_adapter_input[0].T
        )
        active_part, slope_part = silu_parts(gate_activation)
        hidden_state = (active_part * upward_projection).astype(jnp.bfloat16)
        gate_gradient = (hidden_gradient * upward_projection * slope_part).astype(jnp.bfloat16)
        upper_gradient = (hidden_gradient * active_part).astype(jnp.bfloat16)
        gate_backward = exact_product(gate_gradient, gate_adapter_output[0].T)
        upper_backward = exact_product(upper_gradient, upper_adapter_output[0].T)
        reduced_total = exact_product(hidden_state, down_adapter_input[0])
        gate_output_update = ADAPTER_SCALE * exact_product(gate_lowrank.T, gate_gradient)
        upper_output_update = ADAPTER_SCALE * exact_product(upper_lowrank.T, upper_gradient)
        down_input_update = ADAPTER_SCALE * exact_product(hidden_state.T, gradient_lowrank)
        return (
            gate_gradient,
            upper_gradient,
            gate_backward,
            upper_backward,
            reduced_total,
            gate_output_update,
            upper_output_update,
            down_input_update,
        )

    def replicated(normed_all, grad_all, gate_backward, upper_backward, reduced_total):
        gate_input_update = ADAPTER_SCALE * exact_product(normed_all.T, gate_backward)
        upper_input_update = ADAPTER_SCALE * exact_product(normed_all.T, upper_backward)
        down_output_update = ADAPTER_SCALE * exact_product(reduced_total.T, grad_all)
        return (gate_input_update, upper_input_update, down_output_update)

    def rear(left_gate, left_up):
        held_tiles, rows_at, cols_at, active, partner = tile_plans[0]
        summed = tile_product(
            left_gate.reshape(row_count, -1, tile_size),
            held_tiles,
            cols_at,
            rows_at,
            active,
            row_blocks,
            False,
        )
        held_tiles, rows_at, cols_at, active, partner = tile_plans[1]
        summed = summed + tile_product(
            left_up.reshape(row_count, -1, tile_size),
            held_tiles,
            cols_at,
            rows_at,
            active,
            row_blocks,
            False,
        )
        return summed.reshape(row_count, model_width)

    zero_front = tuple(
        (
            jnp.zeros((row_count, col_blocks * fold_count, tile_size), jnp.float32)
            for member in range(3)
        )
    )
    zero_middle = (
        jnp.zeros((row_count, ff_shard), jnp.bfloat16),
        jnp.zeros((row_count, ff_shard), jnp.bfloat16),
        jnp.zeros((row_count, rank_size), jnp.float32),
        jnp.zeros((row_count, rank_size), jnp.float32),
        jnp.zeros((row_count, rank_size), jnp.float32),
        jnp.zeros((rank_size, ff_shard), jnp.float32),
        jnp.zeros((rank_size, ff_shard), jnp.float32),
        jnp.zeros((ff_shard, rank_size), jnp.float32),
    )
    zero_replica = (
        jnp.zeros((model_width, rank_size), jnp.float32),
        jnp.zeros((model_width, rank_size), jnp.float32),
        jnp.zeros((rank_size, model_width), jnp.float32),
    )
    zero_rear = jnp.zeros((row_count, model_width), jnp.float32)
    sums_rep = zero_replica
    sums_shard = zero_middle[5:]
    incoming = jnp.zeros((piece_rows, model_width), jnp.bfloat16)
    produced = jnp.zeros((batch_count, shard_rows, model_width), jnp.bfloat16)
    total_steps = batch_count * piece_count + pipe_size - 1
    for step_index in range(total_steps):
        position = step_index - (pipe_size - 1 - section_now)
        active_step = jnp.logical_and(position >= 0, position < batch_count * piece_count)
        clipped = jnp.clip(position, 0, batch_count * piece_count - 1)
        batch_index = clipped // piece_count
        row_start = clipped % piece_count * piece_rows
        saved = states[0][0]
        given = out_grad[0]
        grad_in = jnp.where(section_now == pipe_size - 1, given, incoming)
        inputs = saved.astype(jnp.float32)
        scale_rms = lax.rsqrt(jnp.mean(inputs * inputs, axis=1, keepdims=True) + EPSILON)
        normed = inputs * scale_rms
        normalized_narrow = (normed * gain_row).astype(jnp.bfloat16)
        normed_all, grad_all = (
            lax.all_gather(normalized_narrow, "tensor", axis=0, tiled=True),
            lax.all_gather(grad_in, "tensor", axis=0, tiled=True),
        )
        gate_matmul, upper_matmul, hidden_matmul = lax.cond(
            active_step, front, lambda *unused: zero_front, normed_all, grad_all
        )
        middle_out = lax.cond(
            active_step,
            middle,
            lambda *unused: zero_middle,
            normed_all,
            grad_all,
            gate_matmul.reshape(row_count, ff_shard),
            upper_matmul.reshape(row_count, ff_shard),
            hidden_matmul.reshape(row_count, ff_shard),
        )
        gate_gradient, upper_gradient, gate_backward, upper_backward, reduced_total = middle_out[:5]
        sums_shard = jax.tree.map(jnp.add, sums_shard, middle_out[5:])
        replica_step = lax.cond(
            active_step,
            replicated,
            lambda *unused: zero_replica,
            normed_all,
            grad_all,
            gate_backward,
            upper_backward,
            reduced_total,
        )
        sums_rep = jax.tree.map(jnp.add, sums_rep, replica_step)
        left_gate = gate_gradient
        left_up = upper_gradient
        running_partial_sum = lax.cond(
            active_step, rear, lambda *unused: zero_rear, left_gate, left_up
        )
        running_partial_sum = running_partial_sum + ADAPTER_SCALE * (
            exact_product(gate_backward, gate_a[0].T) + exact_product(upper_backward, up_a[0].T)
        )
        shared_values = lax.psum_scatter(
            running_partial_sum.astype(jnp.bfloat16), "tensor", scatter_dimension=0, tiled=True
        ).astype(jnp.float32)
        scaled = shared_values * gain_row
        branch = scale_rms * (scaled - normed * jnp.mean(scaled * normed, axis=1, keepdims=True))
        result = (grad_in.astype(jnp.float32) + branch).astype(jnp.bfloat16)
        previous = produced
        produced = lax.dynamic_update_slice(
            produced, jnp.where(active_step, result[None], previous), (batch_index, row_start, 0)
        )
        if step_index + 1 < total_steps:
            incoming = passed_along(result, "pipe", -1)
    sums_rep = lax.psum((sums_rep[0], sums_rep[1], sums_rep[2]), ("tensor", "dp"))
    sums_shard = (
        lax.psum(sums_shard[0].astype(jnp.bfloat16), "dp").astype(jnp.float32),
        lax.psum(sums_shard[1].astype(jnp.bfloat16), "dp").astype(jnp.float32),
        lax.psum(sums_shard[2].astype(jnp.bfloat16), "dp").astype(jnp.float32),
    )
    return (
        produced[None],
        sums_rep[0].astype(jnp.bfloat16)[None],
        sums_shard[0].astype(jnp.bfloat16)[None],
        sums_rep[1].astype(jnp.bfloat16)[None],
        sums_shard[1].astype(jnp.bfloat16)[None],
        sums_shard[2].astype(jnp.bfloat16)[None],
        sums_rep[2].astype(jnp.bfloat16)[None],
    )


def solution(mesh):
    placed = (
        P("pipe", "dp", "tensor", None),
        P("dp", "tensor", None),
        P("pipe", None),
        P("pipe", "tensor", None, None),
        P("pipe", "tensor", None, None),
        P("pipe", "tensor", None, None),
        P("pipe", None, "tensor", None),
        P("pipe", None, "tensor"),
        P("pipe", None, None),
        P("pipe", None, "tensor"),
        P("pipe", None, None),
        P("pipe", None, "tensor"),
        P("pipe", "tensor", None),
        P("pipe", None, None),
    )
    return jax.shard_map(
        shards,
        mesh=mesh,
        in_specs=placed,
        out_specs=(
            P("pipe", "dp", "tensor", None),
            P("pipe", None, None),
            P("pipe", None, "tensor"),
            P("pipe", None, None),
            P("pipe", None, "tensor"),
            P("pipe", "tensor", None),
            P("pipe", None, None),
        ),
        check_vma=False,
    )
```

profile of v0, /device:TPU:1, one launch (start us, length us, event | category | flops | bytes accessed | tf_op | source)
XLA Modules:
  0.0 1686.9 jit_solution(7329547768458717881)
XLA Ops:
  16.1 70.7 %all-gather.13.cloned.1.call-done = bf16[32,4,4096]{2,1,0:T(4,128)(2,1)} async-done(((bf16[1,4,4096]{2,1,0:T(4,128)(2,1)}), bf16[32,4,4096]{2,1,0:T(4,128)(2,1)}) %all-gather.13.cloned.1.call-update) | async-done | bytes 1048592 | tf_op jit(solution)/shard_map/all_gather | solution.py:213
  88.1 75.7 %all-gather.11.cloned.1.call-done = bf16[32,4,4096]{2,1,0:T(4,128)(2,1)} async-done(((bf16[1,4,4096]{2,1,0:T(4,128)(2,1)}), bf16[32,4,4096]{2,1,0:T(4,128)(2,1)}) %all-gather.11.cloned.1.call-update) | async-done | bytes 1048592 | tf_op jit(solution)/shard_map/all_gather | solution.py:214
  165.9 5.4 conditional.16
  172.9 2.4 fusion.394
  175.3 12.8 conditional.18
  188.2 4.3 fusion.380
  193.9 240.9 %all-reduce.13.cloned.1.call-done = bf16[128,4096]{1,0:T(8,128)(2,1)} async-done(((bf16[128,4096]{1,0:T(8,128)(2,1)}), bf16[128,4096]{1,0:T(8,128)(2,1)}) %all-reduce.13.cloned.1.call-update) | async-done | bytes 1048592
  438.7 3.4 collective-permute-done
  443.4 75.0 %all-gather.15.cloned.1.call-done = bf16[32,4,4096]{2,1,0:T(4,128)(2,1)} async-done(((bf16[1,4,4096]{2,1,0:T(4,128)(2,1)}), bf16[32,4,4096]{2,1,0:T(4,128)(2,1)}) %all-gather.15.cloned.1.call-update) | async-done | bytes 1048592 | tf_op jit(solution)/shard_map/all_gather | solution.py:214
  520.6 5.4 conditional.19
  527.6 2.4 fusion.392
  530.0 13.1 conditional.21
  543.1 4.3 fusion.381
  547.5 242.5 %all-reduce.15.cloned.1.call-done = bf16[128,4096]{1,0:T(8,128)(2,1)} async-done(((bf16[128,4096]{1,0:T(8,128)(2,1)}), bf16[128,4096]{1,0:T(8,128)(2,1)}) %all-reduce.15.cloned.1.call-update) | async-done | bytes 1048592
  793.3 3.4 collective-permute-done.1
  798.0 75.0 %all-gather.17.cloned.1.call-done = bf16[32,4,4096]{2,1,0:T(4,128)(2,1)} async-done(((bf16[1,4,4096]{2,1,0:T(4,128)(2,1)}), bf16[32,4,4096]{2,1,0:T(4,128)(2,1)}) %all-gather.17.cloned.1.call-update) | async-done | bytes 1048592 | tf_op jit(solution)/shard_map/all_gather | solution.py:214
  875.1 5.2 conditional.22
  881.9 2.4 fusion.390
  884.3 10.5 conditional.24
  894.8 4.4 fusion.382
  899.3 245.8 %all-reduce.17.cloned.1.call-done = bf16[128,4096]{1,0:T(8,128)(2,1)} async-done(((bf16[128,4096]{1,0:T(8,128)(2,1)}), bf16[128,4096]{1,0:T(8,128)(2,1)}) %all-reduce.17.cloned.1.call-update) | async-done | bytes 1048592
  1148.4 3.4 collective-permute-done.2
  1156.9 3.2 conditional.30
  1160.1 67.9 %all-gather.19.cloned.1.call-done = bf16[32,4,4096]{2,1,0:T(4,128)(2,1)} async-done(((bf16[1,4,4096]{2,1,0:T(4,128)(2,1)}), bf16[32,4,4096]{2,1,0:T(4,128)(2,1)}) %all-gather.19.cloned.1.call-update) | async-done | bytes 1048592 | tf_op jit(solution)/shard_map/all_gather | solution.py:214
  1230.2 62.6 %conditional.25 = (f32[128,640]{0,1:T(8,128)}, f32[128,640]{0,1:T(8,128)}, f32[128,640]{0,1:T(8,128)}) conditional(s32[]{:T(128)} %convert_element_type.223, () %tuple.174, (s32[1,110,1]{1,2,0:T(1,128)}, pred[110]{0:T(512)(128)(4,1)}, bf16[128,4096]{1,0:T(8,128)(2,1)S(1)}, s32[110]{0:T(128)}, bf16[110,128,128]{2,1,0:T(8,128)(2,1)}, ...), branch_computations={%region_25.28_spmd, %region_26.29_spmd} | conditional | flops 1713939712 | bytes 141131904 | solution.py:216
  1234.0 2.9 gather_fusion.16
  1236.9 4.3 fusion.303
  1242.2 7.4 fusion.319
  1253.8 2.5 copy.278
  1256.2 4.1 gather_fusion.17
  1260.4 5.8 fusion.301
  1267.1 7.4 fusion.322
  1276.5 2.9 gather_fusion.15
  1279.4 4.3 fusion.305
  1284.9 6.6 fusion.316
  1292.8 12.5 conditional.26
  1305.4 2.4 fusion.388
  1307.8 41.1 %conditional.27 = (f32[128,4096]{1,0:T(8,128)}) conditional(s32[]{:T(128)} %convert_element_type.223, () %tuple.172, (s32[1,110,1]{1,2,0:T(1,128)}, pred[110]{0:T(512)(128)(4,1)}, bf16[128,640]{1,0:T(8,128)(2,1)}, s32[110]{0:T(128)S(1)}, bf16[110,128,128]{2,1,0:T(8,128)(2,1)}, /*index=5*/s32[1,110,1]{1,2,0:T(1,128)}, pred[110]{0:T(512)(128)(4,1)S(1)}, ...), branch_computations={%region_29.32_spmd, %region_30.33_spmd} | conditional | flops 2311013888 | bytes 106710824 | solution.py:244
  1309.3 2.9 gather_fusion.19
  1312.2 5.8 fusion.347
  1318.9 8.2 fusion.343
  1328.3 2.9 gather_fusion.18
  1331.3 6.0 fusion.349
  1338.8 6.8 fusion.357
  1345.7 3.0 copy.472
  1348.9 4.4 fusion.383
  1365.0 280.8 %all-reduce.22 = (bf16[4096,64]{0,1:T(8,128)(2,1)}, bf16[4096,64]{0,1:T(8,128)(2,1)}, bf16[64,4096]{1,0:T(8,128)(2,1)}) all-reduce(f32[4096,64]{0,1:T(8,128)S(1)} %add_add_fusion.2, f32[4096,64]{0,1:T(8,128)S(1)} %add_add_fusion.1, f32[64,4096]{1,0:T(8,128)S(1)} %add_add_fusion), channel_id=1, replica_groups=mesh['pipe'=4,'tensor'=32,'dp'=2] {'tensor','dp'}, use_global_device_ids=true, to_apply=%region_41.44 | all-reduce | flops 786432 | bytes 4718592 | tf_op jit(solution)/shard_map/psum | solution.py:262
  1648.5 26.5 %all-reduce.21.cloned.1.call-done = (bf16[1,64,640]{2,1,0:T(8,128)(2,1)}, bf16[1,64,640]{2,1,0:T(8,128)(2,1)}, bf16[1,640,64]{1,2,0:T(8,128)(2,1)}) async-done(((bf16[1,64,640]{2,1,0:T(8,128)(2,1)}, bf16[1,64,640]{2,1,0:T(8,128)(2,1)}, bf16[1,640,64]{1,2,0:T(8,128)(2,1)}), (bf16[1,64,640]{2,1,0:T(8,128)(2,1)}, bf16[1,64,640]{2,1,0:T(8,128)(2,1)}, ...) | async-done | bytes 245776 | tf_op jit(solution)/shard_map/psum | solution.py:264
  (352 shorter events, 112.9 us)
Async XLA Ops:
  7.2 79.6 %all-gather.13.cloned.1.call-start = ((), (), s32[]{:S(2)}) async-start(), calls=%async_computation.1 | async-start | bytes 1081344 | tf_op jit(solution)/shard_map/all_gather | solution.py:213
  10.4 153.4 %all-gather.11.cloned.1.call-start = ((), (), s32[]{:S(2)}) async-start(), calls=%async_computation | async-start | bytes 1081344 | tf_op jit(solution)/shard_map/all_gather | solution.py:214
  11.8 423.0 %all-reduce.13.cloned.1.call-start = ((), (), s32[]{:S(2)}) async-start(), calls=%async_computation.5 | async-start | bytes 2097152
  13.9 506.7 %copy-start.89 = (pred[110]{0:T(512)(128)(4,1)}, pred[110]{0:T(512)(128)(4,1)S(1)}, u32[]{:S(2)}) copy-start(pred[110]{0:T(512)(128)(4,1)S(1)} %iota_compare_fusion.22) | copy-start | bytes 334
  15.2 505.4 %copy-start.112 = (pred[110]{0:T(512)(128)(4,1)}, pred[110]{0:T(512)(128)(4,1)S(1)}, u32[]{:S(2)}) copy-start(pred[110]{0:T(512)(128)(4,1)S(1)} %get-tuple-element.1176) | copy-start | bytes 334
  16.0 159.3 %copy-start.95 = (s32[1,110,1]{1,2,0:T(1,128)}, s32[1,110,1]{1,2,0:T(1,128)S(1)}, u32[]{:S(2)}) copy-start(s32[1,110,1]{1,2,0:T(1,128)S(1)} %get-tuple-element.1169) | copy-start | bytes 1324
  16.0 159.3 %copy-start.99 = (s32[1,110,1]{1,2,0:T(1,128)}, s32[1,110,1]{1,2,0:T(1,128)S(1)}, u32[]{:S(2)}) copy-start(s32[1,110,1]{1,2,0:T(1,128)S(1)} %get-tuple-element.1172) | copy-start | bytes 1324
  16.0 504.6 %copy-start.81 = (s32[110]{0:T(128)}, s32[110]{0:T(128)S(1)}, u32[]{:S(2)}) copy-start(s32[110]{0:T(128)S(1)} %get-tuple-element.1166) | copy-start | bytes 1324
  16.0 504.6 %copy-start.85 = (s32[110]{0:T(128)}, s32[110]{0:T(128)S(1)}, u32[]{:S(2)}) copy-start(s32[110]{0:T(128)S(1)} %get-tuple-element.1167) | copy-start | bytes 1324
  16.0 504.6 %copy-start.103 = (s32[1,110,1]{1,2,0:T(1,128)}, s32[1,110,1]{1,2,0:T(1,128)S(1)}, u32[]{:S(2)}) copy-start(s32[1,110,1]{1,2,0:T(1,128)S(1)} %get-tuple-element.1168) | copy-start | bytes 1324
  16.0 504.6 %copy-start.106 = (s32[1,110,1]{1,2,0:T(1,128)}, s32[1,110,1]{1,2,0:T(1,128)S(1)}, u32[]{:S(2)}) copy-start(s32[1,110,1]{1,2,0:T(1,128)S(1)} %get-tuple-element.1170) | copy-start | bytes 1324
  16.1 504.6 %copy-start.109 = (s32[1,110,1]{1,2,0:T(1,128)}, s32[1,110,1]{1,2,0:T(1,128)S(1)}, u32[]{:S(2)}) copy-start(s32[1,110,1]{1,2,0:T(1,128)S(1)} %get-tuple-element.1171) | copy-start | bytes 1324
  16.1 504.6 %copy-start.116 = (s32[110]{0:T(128)}, s32[110]{0:T(128)S(1)}, u32[]{:S(2)}) copy-start(s32[110]{0:T(128)S(1)} %get-tuple-element.1164) | copy-start | bytes 1324
  165.9 5.5 copy-start
  165.9 5.5 copy-start.1
  165.9 5.5 copy-start.10
  165.9 5.5 copy-start.11
  165.9 5.5 copy-start.30
  172.9 15.3 copy-start.55
  188.2 4.5 copy-start.119
  188.2 246.6 %copy-start.28 = (bf16[1,1,4,4096]{3,2,1,0:T(4,128)(2,1)S(1)}, bf16[1,1,4,4096]{3,2,1,0:T(4,128)(2,1)}, u32[]{:S(2)}) copy-start(bf16[1,1,4,4096]{3,2,1,0:T(4,128)(2,1)} %param.50) | copy-start | bytes 98308
  188.2 247.7 %copy-start.29 = (bf16[1,4,4096]{2,1,0:T(4,128)(2,1)S(1)}, bf16[1,4,4096]{2,1,0:T(4,128)(2,1)}, u32[]{:S(2)}) copy-start(bf16[1,4,4096]{2,1,0:T(4,128)(2,1)} %param.51) | copy-start | bytes 98308
  192.6 325.8 %all-gather.15.cloned.1.call-start = ((), (), s32[]{:S(2)}) async-start(), calls=%async_computation.2 | async-start | bytes 1081344 | tf_op jit(solution)/shard_map/all_gather | solution.py:214
  437.4 4.6 collective-permute-start
  443.4 346.6 %all-reduce.15.cloned.1.call-start = ((), (), s32[]{:S(2)}) async-start(), calls=%async_computation.6 | async-start | bytes 2097152
  543.1 248.0 %copy-start.80 = (bf16[4,4096]{1,0:T(4,128)(2,1)S(1)}, bf16[4,4096]{1,0:T(4,128)(2,1)}, u32[]{:S(2)}) copy-start(bf16[4,4096]{1,0:T(4,128)(2,1)} %copy-done.79) | copy-start | bytes 98308
  543.1 332.1 %copy-start.82 = (s32[110]{0:T(128)S(1)}, s32[110]{0:T(128)}, u32[]{:S(2)}) copy-start(s32[110]{0:T(128)} %copy-done.81) | copy-start | bytes 1324
  543.1 332.1 %copy-start.86 = (s32[110]{0:T(128)S(1)}, s32[110]{0:T(128)}, u32[]{:S(2)}) copy-start(s32[110]{0:T(128)} %copy-done.85) | copy-start | bytes 1324
  547.4 325.6 %all-gather.17.cloned.1.call-start = ((), (), s32[]{:S(2)}) async-start(), calls=%async_computation.3 | async-start | bytes 1081344 | tf_op jit(solution)/shard_map/all_gather | solution.py:214
  792.0 83.1 %copy-start.74 = (bf16[4,4096]{1,0:T(4,128)(2,1)}, bf16[4,4096]{1,0:T(4,128)(2,1)S(1)}, u32[]{:S(2)}) copy-start(bf16[4,4096]{1,0:T(4,128)(2,1)S(1)} %fusion.418) | copy-start | bytes 98308
  792.0 4.7 collective-permute-start.1
  798.0 347.1 %all-reduce.17.cloned.1.call-start = ((), (), s32[]{:S(2)}) async-start(), calls=%async_computation.7 | async-start | bytes 2097152
  894.8 258.3 %copy-start.2 = (bf16[128,4096]{1,0:T(8,128)(2,1)S(1)}, bf16[128,4096]{1,0:T(8,128)(2,1)}, u32[]{:S(2)}) copy-start(bf16[128,4096]{1,0:T(8,128)(2,1)} %reshape.512) | copy-start | bytes 3145732
  894.8 258.3 %copy-start.56 = (f32[128,64]{0,1:T(8,128)S(1)}, f32[128,64]{0,1:T(8,128)}, u32[]{:S(2)}) copy-start(f32[128,64]{0,1:T(8,128)} %copy-done.55) | copy-start | bytes 98308
  899.3 328.8 %all-gather.19.cloned.1.call-start = ((), (), s32[]{:S(2)}) async-start(), calls=%async_computation.4 | async-start | bytes 1081344 | tf_op jit(solution)/shard_map/all_gather | solution.py:214
  1147.1 4.7 copy-start.76
  1147.1 4.7 collective-permute-start.2
  1153.0 492.8 %all-reduce.19.cloned.1.call-start = ((), (), s32[]{:S(2)}) async-start(), calls=%async_computation.8 | async-start | bytes 2097152
  1267.1 9.3 copy-start.118
  1348.9 4.5 copy-start.5
  1348.9 4.5 copy-start.69
  1353.4 321.6 %all-reduce.21.cloned.1.call-start = ((), (), s32[]{:S(2)}) async-start(), calls=%async_computation.9 | async-start | bytes 491520 | tf_op jit(solution)/shard_map/psum | solution.py:264
  1355.2 3.8 copy-start.15
  1355.2 3.8 copy-start.21
  1362.9 284.0 %copy-start.71 = (bf16[4,4096]{1,0:T(4,128)(2,1)S(1)}, bf16[4,4096]{1,0:T(4,128)(2,1)}, u32[]{:S(2)}) copy-start(bf16[4,4096]{1,0:T(4,128)(2,1)} %copy-done.70) | copy-start | bytes 98308
  1362.9 284.0 %copy-start.73 = (bf16[4,4096]{1,0:T(4,128)(2,1)S(1)}, bf16[4,4096]{1,0:T(4,128)(2,1)}, u32[]{:S(2)}) copy-start(bf16[4,4096]{1,0:T(4,128)(2,1)} %copy-done.72) | copy-start | bytes 98308
  1362.9 284.0 %copy-start.75 = (bf16[4,4096]{1,0:T(4,128)(2,1)S(1)}, bf16[4,4096]{1,0:T(4,128)(2,1)}, u32[]{:S(2)}) copy-start(bf16[4,4096]{1,0:T(4,128)(2,1)} %copy-done.74) | copy-start | bytes 98308
  1362.9 284.0 %copy-start.77 = (bf16[4,4096]{1,0:T(4,128)(2,1)S(1)}, bf16[4,4096]{1,0:T(4,128)(2,1)}, u32[]{:S(2)}) copy-start(bf16[4,4096]{1,0:T(4,128)(2,1)} %copy-done.76) | copy-start | bytes 98308
  (62 other events, 125.8 us)
Sparse Core Ops, SparseCore 0:
  11.2 75.5 all-gather.12
  89.9 73.7 all-gather.10
  192.7 242.0 all-reduce.12
  443.5 74.8 all-gather.14
  547.6 242.3 all-reduce.14
  798.1 74.8 all-gather.16
  899.4 245.6 all-reduce.16
  1153.1 74.8 all-gather.18
  1353.5 144.5 all-reduce.18
  1645.9 29.0 all-reduce.20
where the time goes:
time: 1700 us; the launch traced here: 1690 us
  waiting for transfers between devices  1130 us (66%)
  blocking collectives  281 us (17%)
  matrix products  100 us (6%)
  local copies, waits for them, and re-layouts  87.1 us (5%)
  loops' own time  42.7 us (3%)
  other arithmetic  25.2 us (1%)
    unnamed x14, waiting for transfers between devices  729 us
    all_gather x4, waiting for transfers between devices, shards(): lax.all_gather(grad_in, 'tensor', axis=0, tiled=True)  294 us
    psum x1, blocking collectives, shards(): lax.psum((sums_rep[0], sums_rep[1], sums_rep[2]), ('tensor', 'dp'))  281 us
    all_gather x1, waiting for transfers between devices, shards(): lax.all_gather(normalized_narrow, 'tensor', axis=0, tiled=True)  70.7 us
    dot_general x23, matrix products, exact_product(): jnp.dot(left.astype(jnp.float32), right.astype(jnp.float32), precision=EX...  37.7 us
    dot_general x5, matrix products, tile_product(): jnp.dot(routing, product.reshape(slots, -1), precision=EXACT_PRECISION)  36.4 us
  transfers between devices with their start and end apart: 13, of which 12 were waited for; matrix products, arithmetic and copies ran while one was open for 1% of the time, Pallas kernels for 0%

commit v1 on v0

v1 whole, which is shorter than its diff:
```python
import functools

import jax
import jax.numpy as jnp
from jax import lax
from jax.experimental import pallas as pl
from jax.experimental.pallas import tpu as pltpu
from jax.sharding import PartitionSpec as P

MESH = pl.DeviceIdType.MESH
F32 = jnp.float32
BF16 = jnp.bfloat16
EPSILON = 1e-05
SCALE = 0.25
X_CHIPS = 4
TILE = 128
EXTRA = 256


def dot_nn(a, b):
    return lax.dot_general(a, b, (((1,), (0,)), ((), ())), preferred_element_type=F32)


def dot_nt(a, b):
    return lax.dot_general(a, b, (((1,), (1,)), ((), ())), preferred_element_type=F32)


def dot_tn(a, b):
    return lax.dot_general(a, b, (((0,), (0,)), ((), ())), preferred_element_type=F32)


def each(count, body):
    def step(i, carry):
        body(i)
        return carry

    lax.fori_loop(0, count, step, 0)


def aligned(index, size):
    return pl.ds(pl.multiple_of(index * size, size), size)


def section_kernel(
    sizes,
    inv,
    x_ref,
    go_ref,
    gain_ref,
    gate_hbm,
    up_hbm,
    down_hbm,
    ab_hbm,
    gb_ref,
    ub_ref,
    da_ref,
    db_hbm,
    dx_out,
    ab_out,
    hid_out,
    da_out,
    db_out,
    tiles_g,
    tiles_u,
    tiles_d,
    wg,
    wu,
    wd,
    gbx,
    ubx,
    dax,
    a2a_send,
    a2a_recv,
    n16,
    r16,
    u_all,
    g_all,
    acc_g,
    acc_u,
    acc_d,
    a_gu,
    c_lr,
    hid,
    dge,
    dup,
    tm,
    slab_send,
    slab_recv,
    total,
    z_send,
    z_recv,
    dx16,
    dx32,
    o_send,
    o_recv,
    t_all,
    pa_send,
    pa_recv,
    pb_send,
    pb_recv,
    ps_send,
    ps_recv,
    pd_send,
    pd_recv,
    load_sem,
    a2a_ss,
    a2a_rs,
    uz_ss,
    uz_rs,
    ux_ss,
    ux_rs,
    gz_ss,
    gz_rs,
    gx_ss,
    gx_rs,
    y_ss,
    y_rs,
    rx_ss,
    rx_rs,
    rz_ss,
    rz_rs,
    o_ss,
    o_rs,
    tz_ss,
    tz_rs,
    dp_ss,
    dp_rs,
):
    pipe_n, nz, nx, hidden, width = sizes
    slab = width // nx
    rows_q = x_ref.shape[0]
    zt = rows_q * nx
    col_blocks = hidden // TILE
    row_blocks = width // TILE
    rank = gb_ref.shape[0]
    pipe = lax.axis_index("pipe")
    tensor = lax.axis_index("tensor")
    core = lax.axis_index("dp")
    z = tensor // nx
    x = lax.rem(tensor, nx)

    def remote(src, dst, ss, rs, **where):
        return pltpu.make_async_remote_copy(
            src_ref=src, dst_ref=dst, send_sem=ss, recv_sem=rs, device_id=where, device_id_type=MESH
        )

    def x_peer(i):
        return z * nx + lax.rem(x + i, nx)

    def z_peer(i):
        return lax.rem(z + i, nz) * nx + x

    barrier = pltpu.get_barrier_semaphore()

    def greet(**where):
        pl.semaphore_signal(barrier, inc=1, device_id=where, device_id_type=MESH)

    each(nx - 1, lambda i: greet(tensor=x_peer(i + 1)))
    each(nz - 1, lambda i: greet(tensor=z_peer(i + 1)))
    greet(dp=1 - core)
    greet(pipe=lax.rem(pipe + 1, pipe_n))
    greet(pipe=lax.rem(pipe + pipe_n - 1, pipe_n))

    loads = [
        pltpu.make_async_copy(gate_hbm, tiles_g, load_sem.at[0]),
        pltpu.make_async_copy(up_hbm, tiles_u, load_sem.at[1]),
        pltpu.make_async_copy(down_hbm, tiles_d, load_sem.at[2]),
        pltpu.make_async_copy(ab_hbm, wg.at[:, pl.ds(hidden, TILE)], load_sem.at[3]),
        pltpu.make_async_copy(db_hbm, wd.at[pl.ds(hidden, rank), :], load_sem.at[4]),
    ]
    for load in loads:
        load.start()

    xin = x_ref[...].astype(F32)
    scale_rms = lax.rsqrt(jnp.mean(xin * xin, axis=1, keepdims=True) + EPSILON)
    normed = xin * scale_rms
    given = go_ref[...].astype(F32)
    for k in range(nx):
        a2a_send[k, :, 0:slab] = normed[:, k * slab : (k + 1) * slab]
        a2a_send[k, :, slab : 2 * slab] = given[:, k * slab : (k + 1) * slab]
        a2a_send[k, :, 2 * slab : 2 * slab + TILE] = jnp.broadcast_to(scale_rms, (rows_q, TILE))

    pl.semaphore_wait(barrier, (nx - 1) + (nz - 1) + 3)

    def a2a(i):
        return remote(
            a2a_send.at[lax.rem(x + i + 1, nx)],
            a2a_recv.at[x],
            a2a_ss.at[i],
            a2a_rs.at[i],
            tensor=x_peer(i + 1),
        )

    each(nx - 1, lambda i: a2a(i).start())
    a2a_recv[x] = a2a_send[x]
    each(nx - 1, lambda i: a2a(i).wait())
    for k in range(nx):
        n16[k * rows_q : (k + 1) * rows_q, :] = a2a_recv[k, :, 0:slab]
        dx32[k * rows_q : (k + 1) * rows_q, :] = a2a_recv[k, :, slab : 2 * slab]
        r16[k * rows_q : (k + 1) * rows_q, :] = a2a_recv[k, :, 2 * slab : 2 * slab + TILE]
    gain = gain_ref[:, aligned(x, slab)].astype(F32)
    mine = aligned(z, zt)
    u_all[x, mine, :] = (n16[...] * gain).astype(BF16)

    def gather_z(buf, ss, rs, i):
        return remote(
            buf.at[x, mine], buf.at[x, mine], ss.at[i], rs.at[i], tensor=z_peer(i + 1)
        )

    def gather_x(buf, ss, rs, i):
        return remote(buf.at[x], buf.at[x], ss.at[i], rs.at[i], tensor=x_peer(i + 1))

    def u_z(i):
        return gather_z(u_all, uz_ss, uz_rs, i)

    def u_x(i):
        return gather_x(u_all, ux_ss, ux_rs, i)

    def g_z(i):
        return gather_z(g_all, gz_ss, gz_rs, i)

    def g_x(i):
        return gather_x(g_all, gx_ss, gx_rs, i)

    last = pipe == pipe_n - 1

    each(nz - 1, lambda i: u_z(i).start())

    @pl.when(last)
    def _():
        g_all[x, mine, :] = dx32[...].astype(BF16)
        each(nz - 1, lambda i: g_z(i).start())

    gbx[...] = jnp.zeros_like(gbx)
    ubx[...] = jnp.zeros_like(ubx)
    dax[...] = jnp.zeros_like(dax)
    gbx[0:rank, :] = gb_ref[...]
    ubx[rank : 2 * rank, :] = ub_ref[...]
    dax[:, 0:rank] = da_ref[...]
    wd[hidden + rank : hidden + TILE, :] = jnp.zeros((TILE - rank, width), BF16)

    def placed(tiles, member, block):
        slot = inv[member, block]
        tile = tiles[jnp.maximum(slot, 0)]
        return jnp.where(slot >= 0, tile, jnp.zeros_like(tile))

    loads[0].wait()

    def build_gate(r):
        for c in range(col_blocks):
            wg[aligned(r, TILE), c * TILE : (c + 1) * TILE] = placed(tiles_g, 0, r * col_blocks + c)

    each(row_blocks, build_gate)
    each(nz - 1, lambda i: u_z(i).wait())
    each(nx - 1, lambda i: u_x(i).start())

    @pl.when(last)
    def _():
        each(nz - 1, lambda i: g_z(i).wait())
        each(nx - 1, lambda i: g_x(i).start())

    loads[1].wait()

    def build_up(r):
        for c in range(col_blocks):
            wu[aligned(r, TILE), c * TILE : (c + 1) * TILE] = placed(tiles_u, 1, r * col_blocks + c)

    each(row_blocks, build_up)
    loads[2].wait()

    def build_down(c):
        for r in range(col_blocks):
            wd[r * TILE : (r + 1) * TILE, aligned(c, TILE)] = placed(tiles_d, 2, r * row_blocks + c)

    each(row_blocks, build_down)
    loads[3].wait()
    loads[4].wait()

    each(nx - 1, lambda i: u_x(i).wait())
    acc_g[...] = jnp.zeros_like(acc_g)
    acc_u[...] = jnp.zeros_like(acc_u)

    def forward(k):
        rows = aligned(k, slab)
        acc_g[...] += dot_nn(u_all[k], wg[rows, :])
        acc_u[...] += dot_nn(u_all[k], wu[rows, :])

    each(nx, forward)
    a_gu[...] = acc_g[:, hidden : hidden + TILE].astype(BF16)
    acc_g[:, 0:hidden] += SCALE * dot_nn(a_gu[...], gbx[...])
    acc_u[...] += SCALE * dot_nn(a_gu[...], ubx[...])

    @pl.when(jnp.logical_not(last))
    def _():
        remote(
            dx16, g_all.at[x, mine], y_ss.at[0], y_rs.at[0], pipe=lax.rem(pipe + 1, pipe_n)
        ).wait_recv()
        each(nz - 1, lambda i: g_z(i).start())
        each(nz - 1, lambda i: g_z(i).wait())
        each(nx - 1, lambda i: g_x(i).start())

    each(nx - 1, lambda i: g_x(i).wait())

    acc_d[...] = jnp.zeros_like(acc_d)

    def hidden_grad(k):
        acc_d[...] += dot_nt(g_all[k], wd[:, aligned(k, slab)])

    each(nx, hidden_grad)
    c_lr[...] = acc_d[:, hidden : hidden + TILE].astype(BF16)
    acc_d[:, 0:hidden] += SCALE * dot_nt(c_lr[...], dax[...])

    lane = lax.broadcasted_iota(jnp.int32, (zt, TILE), 1)

    def middle(j):
        rows = aligned(j, zt)
        gate = acc_g[rows, 0:hidden]
        up = acc_u[rows, :]
        dh = acc_d[rows, 0:hidden]
        q = jax.nn.sigmoid(gate)
        active = gate * q
        hid[rows, :] = (active * up).astype(BF16)
        dgate = (dh * up * (q * (1.0 + gate * (1.0 - q)))).astype(BF16)
        dupw = (dh * active).astype(BF16)
        dge[rows, 0:hidden] = dgate
        dup[rows, :] = dupw
        dots = jnp.sum(dgate.astype(F32) * gate + dupw.astype(F32) * up, axis=1, keepdims=True)
        tm[rows, TILE : 2 * TILE] = jnp.where(lane == rank, dots, 0.0)

    each(nz, middle)
    tm[:, 0:TILE] = dot_nt(dge[:, 0:hidden], gbx[...]) + dot_nt(dup[...], ubx[...])
    tm[:, TILE : 2 * TILE] += dot_nn(hid[...], dax[...])
    dge[:, hidden : hidden + TILE] = (SCALE * tm[:, 0:TILE]).astype(BF16)

    def slab_copy(i):
        return remote(
            slab_send.at[i], slab_recv.at[i], rx_ss.at[i], rx_rs.at[i], tensor=x_peer(i + 1)
        )

    def partial(k):
        rows = aligned(k, slab)
        return dot_nt(dge[...], wg[rows, :]) + dot_nt(dup[...], wu[rows, :])

    def send_slab(i):
        slab_send[i, :, 0:slab] = partial(lax.rem(x + i + 1, nx)).astype(BF16)
        slab_send[i, :, slab : slab + EXTRA] = tm[...].astype(BF16)
        slab_copy(i).start()

    each(nx - 1, send_slab)
    total[:, 0:slab] = partial(x)
    total[:, slab : slab + EXTRA] = tm[...]

    ps_send[0:rank, :] = (SCALE * dot_tn(a_gu[...], dge[:, 0:hidden]))[0:rank, :].astype(BF16)
    ps_send[rank : 2 * rank, :] = (SCALE * dot_tn(a_gu[...], dup[...]))[rank : 2 * rank, :].astype(BF16)
    pd_send[...] = (SCALE * dot_tn(hid[...], c_lr[...])).astype(BF16)

    def swap(src, dst, i):
        return remote(src, dst, dp_ss.at[i], dp_rs.at[i], dp=1 - core)

    swap(ps_send, ps_recv, 0).start()
    swap(pd_send, pd_recv, 1).start()

    each(nx - 1, lambda i: slab_copy(i).wait())

    def add_slabs(j):
        rows = aligned(j, zt)
        value = total[rows, :]
        for i in range(nx - 1):
            value = value + slab_recv[i, rows, :].astype(F32)
        total[rows, :] = value
        z_send[rows, :] = value.astype(BF16)

    each(nz, add_slabs)

    def z_copy(i):
        return remote(
            z_send.at[aligned(lax.rem(z + i + 1, nz), zt)],
            z_recv.at[i],
            rz_ss.at[i],
            rz_rs.at[i],
            tensor=z_peer(i + 1),
        )

    each(nz - 1, lambda i: z_copy(i).start())
    each(nz - 1, lambda i: z_copy(i).wait())
    value = total[mine, :]
    for i in range(nz - 1):
        value = value + z_recv[i].astype(F32)

    zm = value[:, slab + TILE : slab + 2 * TILE]
    mean = jnp.sum(jnp.where(lane == rank, zm, 0.0), axis=1, keepdims=True) / width
    dn = value[:, 0:slab] * gain
    row_scale = r16[:, 0:1]
    dx = g_all[x, mine, :].astype(F32) + row_scale * (dn - n16[...] * mean)
    dx16[...] = dx.astype(BF16)

    def y_copy():
        return remote(
            dx16, g_all.at[x, mine], y_ss.at[0], y_rs.at[0], pipe=lax.rem(pipe + pipe_n - 1, pipe_n)
        )

    @pl.when(pipe > 0)
    def _():
        y_copy().start()

    t_all[mine, :] = value[:, slab : slab + EXTRA].astype(BF16)

    def t_z(i):
        return remote(
            t_all.at[mine], t_all.at[mine], tz_ss.at[i], tz_rs.at[i], tensor=z_peer(i + 1)
        )

    each(nz - 1, lambda i: t_z(i).start())

    dx32[...] = dx16[...].astype(F32)
    for k in range(nx):
        o_send[k] = dx32[k * rows_q : (k + 1) * rows_q, :]

    def o_copy(i):
        return remote(
            o_send.at[lax.rem(x + i + 1, nx)],
            o_recv.at[x],
            o_ss.at[i],
            o_rs.at[i],
            tensor=x_peer(i + 1),
        )

    each(nx - 1, lambda i: o_copy(i).start())
    o_recv[x] = o_send[x]

    swap(ps_send, ps_recv, 0).wait()
    swap(pd_send, pd_recv, 1).wait()
    hid_out[...] = (ps_send[...].astype(F32) + ps_recv[...].astype(F32)).astype(BF16)
    da_out[...] = (pd_send[...].astype(F32) + pd_recv[...].astype(F32)).astype(BF16)

    each(nx - 1, lambda i: o_copy(i).wait())
    for k in range(nx):
        dx_out[:, k * slab : (k + 1) * slab] = o_recv[k].astype(BF16)

    each(nz - 1, lambda i: t_z(i).wait())

    def wide(k):
        pa_send[aligned(k, slab), :] = (SCALE * dot_tn(u_all[k], t_all[:, 0:TILE])).astype(BF16)
        pb_send[:, aligned(k, slab)] = (
            SCALE * dot_tn(t_all[:, TILE : 2 * TILE], g_all[k])
        )[0:rank, :].astype(BF16)

    each(nx, wide)
    swap(pa_send, pa_recv, 2).start()
    swap(pb_send, pb_recv, 3).start()
    swap(pa_send, pa_recv, 2).wait()
    swap(pb_send, pb_recv, 3).wait()

    def wide_out(k):
        rows = aligned(k, slab)
        ab_out[rows, :] = (pa_send[rows, :].astype(F32) + pa_recv[rows, :].astype(F32)).astype(BF16)
        db_out[:, rows] = (pb_send[:, rows].astype(F32) + pb_recv[:, rows].astype(F32)).astype(BF16)

    each(nx, wide_out)

    @pl.when(pipe > 0)
    def _():
        y_copy().wait_send()


def shards(
    states,
    out_grad,
    norm_gain,
    gate_tiles,
    up_tiles,
    down_tiles,
    tile_lists,
    tile_counts,
    gate_a,
    gate_adapter_output,
    up_a,
    upper_adapter_output,
    down_adapter_input,
    down_b,
):
    pipe_n = lax.axis_size("pipe")
    tensor_n = lax.axis_size("tensor")
    nx = X_CHIPS
    nz = tensor_n // nx
    rows_q, width = states.shape[2:]
    slots = gate_tiles.shape[1]
    rank = gate_a.shape[2]
    hidden = gate_adapter_output.shape[2]
    tokens = rows_q * tensor_n
    zt = rows_q * nx
    slab = width // nx
    row_blocks, col_blocks = width // TILE, hidden // TILE
    blocks = row_blocks * col_blocks

    places = tile_lists[0]
    strides = jnp.array([col_blocks, col_blocks, row_blocks], jnp.int32)[:, None]
    place = places[:, :, 0] * strides + places[:, :, 1]
    slot_ids = jnp.arange(slots, dtype=jnp.int32)
    alive = slot_ids[None, :] < tile_counts[0]
    hit = jnp.logical_and(
        place[:, None, :] == jnp.arange(blocks, dtype=jnp.int32)[None, :, None], alive[:, None, :]
    )
    inv = jnp.max(jnp.where(hit, slot_ids[None, None, :], -1), axis=2)
    ab = jnp.concatenate([gate_a[0], up_a[0]], axis=1)

    vmem = pl.BlockSpec(memory_space=pltpu.VMEM)
    anywhere = pl.BlockSpec(memory_space=pl.ANY)
    smem = pl.BlockSpec(memory_space=pltpu.SMEM)
    dma = pltpu.SemaphoreType.DMA
    ext = hidden + TILE
    scratch = [
        pltpu.VMEM((slots, TILE, TILE), BF16),
        pltpu.VMEM((slots, TILE, TILE), BF16),
        pltpu.VMEM((slots, TILE, TILE), BF16),
        pltpu.VMEM((width, ext), BF16),
        pltpu.VMEM((width, hidden), BF16),
        pltpu.VMEM((ext, width), BF16),
        pltpu.VMEM((TILE, hidden), BF16),
        pltpu.VMEM((TILE, hidden), BF16),
        pltpu.VMEM((hidden, TILE), BF16),
        pltpu.VMEM((nx, rows_q, 2 * slab + TILE), F32),
        pltpu.VMEM((nx, rows_q, 2 * slab + TILE), F32),
        pltpu.VMEM((zt, slab), F32),
        pltpu.VMEM((zt, TILE), F32),
        pltpu.VMEM((nx, tokens, slab), BF16),
        pltpu.VMEM((nx, tokens, slab), BF16),
        pltpu.VMEM((tokens, ext), F32),
        pltpu.VMEM((tokens, hidden), F32),
        pltpu.VMEM((tokens, ext), F32),
        pltpu.VMEM((tokens, TILE), BF16),
        pltpu.VMEM((tokens, TILE), BF16),
        pltpu.VMEM((tokens, hidden), BF16),
        pltpu.VMEM((tokens, ext), BF16),
        pltpu.VMEM((tokens, hidden), BF16),
        pltpu.VMEM((tokens, EXTRA), F32),
        pltpu.VMEM((nx - 1, tokens, slab + EXTRA), BF16),
        pltpu.VMEM((nx - 1, tokens, slab + EXTRA), BF16),
        pltpu.VMEM((tokens, slab + EXTRA), F32),
        pltpu.VMEM((tokens, slab + EXTRA), BF16),
        pltpu.VMEM((nz - 1, zt, slab + EXTRA), BF16),
        pltpu.VMEM((zt, slab), BF16),
        pltpu.VMEM((zt, slab), F32),
        pltpu.VMEM((nx, rows_q, slab), F32),
        pltpu.VMEM((nx, rows_q, slab), F32),
        pltpu.VMEM((tokens, EXTRA), BF16),
        pltpu.VMEM((width, TILE), BF16),
        pltpu.VMEM((width, TILE), BF16),
        pltpu.VMEM((rank, width), BF16),
        pltpu.VMEM((rank, width), BF16),
        pltpu.VMEM((2 * rank, hidden), BF16),
        pltpu.VMEM((2 * rank, hidden), BF16),
        pltpu.VMEM((hidden, TILE), BF16),
        pltpu.VMEM((hidden, TILE), BF16),
        dma((5,)),
    ]
    for count in (nx - 1, nz - 1, nx - 1, nz - 1, nx - 1, 1, nx - 1, nz - 1, nx - 1, nz - 1, 4):
        scratch += [dma((count,)), dma((count,))]
    dx, ab_grad, hid_grad, da_grad, db_grad = pl.pallas_call(
        functools.partial(section_kernel, (pipe_n, nz, nx, hidden, width)),
        out_shape=(
            jax.ShapeDtypeStruct((rows_q, width), BF16),
            jax.ShapeDtypeStruct((width, 2 * rank), BF16),
            jax.ShapeDtypeStruct((2 * rank, hidden), BF16),
            jax.ShapeDtypeStruct((hidden, TILE), BF16),
            jax.ShapeDtypeStruct((rank, width), BF16),
        ),
        in_specs=[smem, vmem, vmem, vmem] + [anywhere] * 4 + [vmem] * 3 + [anywhere],
        out_specs=[vmem] * 5,
        scratch_shapes=scratch,
        compiler_params=pltpu.CompilerParams(
            collective_id=0, has_side_effects=True, vmem_limit_bytes=56 * 1024 * 1024
        ),
        cost_estimate=pl.CostEstimate(
            flops=10 * tokens * width * hidden,
            bytes_accessed=6 * slots * TILE * TILE,
            transcendentals=tokens * hidden,
        ),
    )(
        inv,
        states[0, 0],
        out_grad[0],
        norm_gain,
        gate_tiles[0],
        up_tiles[0],
        down_tiles[0],
        ab,
        gate_adapter_output[0],
        upper_adapter_output[0],
        down_adapter_input[0],
        down_b[0],
    )
    return (
        dx[None, None],
        ab_grad[None, :, :rank],
        hid_grad[None, :rank],
        ab_grad[None, :, rank:],
        hid_grad[None, rank:],
        da_grad[None, :, :rank],
        db_grad[None],
    )


def solution(mesh):
    placed = (
        P("pipe", "dp", "tensor", None),
        P("dp", "tensor", None),
        P("pipe", None),
        P("pipe", "tensor", None, None),
        P("pipe", "tensor", None, None),
        P("pipe", "tensor", None, None),
        P("pipe", None, "tensor", None),
        P("pipe", None, "tensor"),
        P("pipe", None, None),
        P("pipe", None, "tensor"),
        P("pipe", None, None),
        P("pipe", None, "tensor"),
        P("pipe", "tensor", None),
        P("pipe", None, None),
    )
    return jax.shard_map(
        shards,
        mesh=mesh,
        in_specs=placed,
        out_specs=(
            P("pipe", "dp", "tensor", None),
            P("pipe", None, None),
            P("pipe", None, "tensor"),
            P("pipe", None, None),
            P("pipe", None, "tensor"),
            P("pipe", "tensor", None),
            P("pipe", None, None),
        ),
        check_vma=False,
    )
```

time: 1700 us -> 256 us (0.15)
  waiting for transfers between devices: 1130 us -> 0 us
  blocking collectives: 281 us -> 0 us
  Pallas kernels: 0 us -> 237 us
  matrix products: 100 us -> 0 us
  local copies, waits for them, and re-layouts: 87.1 us -> 14.5 us
  loops' own time: 42.7 us -> 0 us
  other arithmetic: 25.2 us -> 3.78 us
    unnamed x14 -> x0, waiting for transfers between devices: 729 us -> none
    all_gather x5 -> x0, waiting for transfers between devices: 364 us -> none  [the longest x4 294 us: shards(): lax.all_gather(grad_in, 'tensor', axis=0, tiled=True)]
    psum x1 -> x0, blocking collectives: 281 us -> none  [shards(): lax.psum((sums_rep[0], sums_rep[1], sums_rep[2]), ('tensor', 'dp'))]
    pallas_call x0 -> x1, Pallas kernels: none -> 237 us  [shards(): pl.pallas_call(functools.partial(section_kernel, (pipe_n, nz, nx, hidden,...]
    dot_general x33 -> x0, matrix products: 100 us -> none  [the longest x23 37.7 us: exact_product(): jnp.dot(left.astype(jnp.float32), right.astype(jnp.float32), precision=EX...]
    another operation x16 -> x0, loops' own time: 42.7 us -> none  [the longest x4 32.3 us: shards(): lax.cond(active_step, rear, lambda *unused: zero_rear, left_gate, left_up)]
    psum x1 -> x0, waiting for transfers between devices: 26.5 us -> none  [shards(): lax.psum(sums_shard[0].astype(jnp.bfloat16), 'dp').astype(jnp.float32)]
  transfers between devices with their start and end apart: 13 -> 0, of which waited for: 12 -> 0; matrix products, arithmetic and copies ran while one was open for 1% -> 0% of each run, Pallas kernels for 0% -> 0%
where the time goes in v1:
time: 256 us
  Pallas kernels  237 us (93%)
  local copies, waits for them, and re-layouts  14.5 us (6%)
  other arithmetic  3.78 us (1%)
    pallas_call x1, Pallas kernels, shards(): pl.pallas_call(functools.partial(section_kernel, (pipe_n, nz, nx, hidden,...  237 us
    unnamed x12, local copies, waits for them, and re-layouts  9.15 us

profile of v1, /device:TPU:1, one launch (start us, length us, event | category | flops | bytes accessed | tf_op | source)
XLA Modules:
  0.0 255.5 jit_solution(9316448089983351456)
XLA Ops:
  0.6 0.7 iota_compare_fusion.1
  1.4 0.8 fusion.3
  2.1 0.7 fusion.2
  2.8 0.8 select_reduce_fusion.inv
  3.6 1.7 copy.32
  5.3 1.5 copy.30
  6.8 1.5 copy.31
  8.4 1.5 pad_maximum_fusion.ab_hbm
  9.9 236.6 %shard_map.198 = (bf16[4,4096]{1,0:T(4,128)(2,1)}, bf16[4096,128]{1,0:T(8,128)(2,1)}, bf16[128,640]{1,0:T(8,128)(2,1)}, bf16[640,128]{1,0:T(8,128)(2,1)}, bf16[64,4096]{1,0:T(8,128)(2,1)}) custom-call(s32[3,160]{1,0:T(4,128)} %select_reduce_fusion.inv, bf16[4,4096]{1,0:T(4,128)(2,1)} %bitcast.43, bf16[4,4096]{1,0:T(4,128)(2,1)} %bitcast.44, ...), custom_call_target="tpu_custom_call" | custom-call | flops 3355443200 | bytes 10813440 | tf_op jit(solution)/shard_map/pallas_call | solution.py:559
  246.5 0.9 slice_bitcast_fusion.2
  247.4 0.8 copy.35
  248.2 1.6 slice_bitcast_fusion.3
  249.8 0.0 copy-start.1
  249.8 0.0 copy-start
  249.8 2.0 slice_bitcast_fusion
  251.9 1.1 copy.34
  253.0 1.1 copy.33
  254.1 0.0 copy-done.1
  254.1 0.6 copy.46
  254.7 0.0 copy-done
  254.7 0.8 copy.47
Async XLA Ops:
  249.8 4.3 %copy-start.1 = (bf16[4,4096]{1,0:T(4,128)(2,1)S(1)}, bf16[4,4096]{1,0:T(4,128)(2,1)}, u32[]{:S(2)}) copy-start(bf16[4,4096]{1,0:T(4,128)(2,1)} %get-tuple-element.12) | copy-start | bytes 98308
  249.8 4.9 %copy-start = (bf16[64,4096]{1,0:T(8,128)(2,1)S(1)}, bf16[64,4096]{1,0:T(8,128)(2,1)}, u32[]{:S(2)}) copy-start(bf16[64,4096]{1,0:T(8,128)(2,1)} %get-tuple-element.16) | copy-start | bytes 1572868

commit v2 on v1

v2 whole, which is shorter than its diff:
```python
import functools

import jax
import jax.numpy as jnp
from jax import lax
from jax.experimental import pallas as pl
from jax.experimental.pallas import tpu as pltpu
from jax.sharding import PartitionSpec as P

MESH = pl.DeviceIdType.MESH
F32 = jnp.float32
BF16 = jnp.bfloat16
EPSILON = 1e-05
SCALE = 0.25
X_CHIPS = 4
TILE = 128
EXTRA = 256


def dot_nn(a, b):
    return lax.dot_general(a, b, (((1,), (0,)), ((), ())), preferred_element_type=F32)


def dot_nt(a, b):
    return lax.dot_general(a, b, (((1,), (1,)), ((), ())), preferred_element_type=F32)


def dot_tn(a, b):
    return lax.dot_general(a, b, (((0,), (0,)), ((), ())), preferred_element_type=F32)


def each(count, body):
    def step(i, carry):
        body(i)
        return carry

    lax.fori_loop(0, count, step, 0)


def aligned(index, size):
    return pl.ds(pl.multiple_of(index * size, size), size)


def section_kernel(
    sizes,
    inv,
    x_ref,
    go_ref,
    gain_ref,
    gate_hbm,
    up_hbm,
    down_hbm,
    ga_hbm,
    ua_hbm,
    db_hbm,
    gb_ref,
    ub_ref,
    da_ref,
    dx_out,
    wide_own,
    wide_recv,
    hid_own,
    hid_recv,
    tiles_g,
    tiles_u,
    tiles_d,
    wgu,
    wd,
    ab,
    gub,
    dax,
    a2a_send,
    a2a_recv,
    n16,
    r16,
    dx32,
    dx16,
    u_all,
    g_all,
    acc_gu,
    acc_a,
    acc_d,
    a_gu,
    c_lr,
    hid,
    dgu,
    ta,
    tm,
    m_send,
    m_recv,
    s_far,
    r_far,
    s_near,
    r_near,
    total,
    z_send,
    z_recv,
    o_send,
    o_recv,
    t_send,
    t_recv,
    tz_send,
    tz_recv,
    t_all,
    load_sem,
    a2a_ss,
    a2a_rs,
    uz_ss,
    uz_rs,
    ud_ss,
    ud_rs,
    ur_ss,
    ur_rs,
    gz_ss,
    gz_rs,
    gd_ss,
    gd_rs,
    gr_ss,
    gr_rs,
    m_ss,
    m_rs,
    far_ss,
    far_rs,
    near_ss,
    near_rs,
    rz_ss,
    rz_rs,
    o_ss,
    o_rs,
    tx_ss,
    tx_rs,
    tr_ss,
    tr_rs,
    ta_ss,
    ta_rs,
    dp_ss,
    dp_rs,
):
    pipe_n, nz, nx, hidden, width = sizes
    slab = width // nx
    half = slab // 2
    quarter = slab // 4
    rows_q = x_ref.shape[0]
    zt = rows_q * nx
    col_blocks = hidden // TILE
    row_blocks = width // TILE
    rank = gb_ref.shape[0]
    pipe = lax.axis_index("pipe")
    tensor = lax.axis_index("tensor")
    core = lax.axis_index("dp")
    z = tensor // nx
    x = lax.rem(tensor, nx)
    last = pipe == pipe_n - 1
    below = lax.rem(pipe + pipe_n - 1, pipe_n)
    above = lax.rem(pipe + 1, pipe_n)
    right = lax.rem(x + 1, nx)
    left = lax.rem(x + nx - 1, nx)
    across = lax.rem(x + 2, nx)

    def remote(src, dst, ss, rs, **where):
        return pltpu.make_async_remote_copy(
            src_ref=src, dst_ref=dst, send_sem=ss, recv_sem=rs, device_id=where, device_id_type=MESH
        )

    def x_peer(i):
        return z * nx + lax.rem(x + i, nx)

    def z_peer(i):
        return lax.rem(z + i, nz) * nx + x

    def side_peer(side):
        return z * nx + (right if side == 0 else left)

    barrier = pltpu.get_barrier_semaphore()

    def greet(**where):
        pl.semaphore_signal(barrier, inc=1, device_id=where, device_id_type=MESH)

    each(nx - 1, lambda i: greet(tensor=x_peer(i + 1)))
    each(nz - 1, lambda i: greet(tensor=z_peer(i + 1)))
    greet(dp=1 - core)
    each(nz, lambda i: greet(pipe=above, tensor=z_peer(i)))
    each(nz, lambda i: greet(pipe=below, tensor=z_peer(i)))

    loads = [
        pltpu.make_async_copy(gate_hbm, tiles_g, load_sem.at[0]),
        pltpu.make_async_copy(up_hbm, tiles_u, load_sem.at[1]),
        pltpu.make_async_copy(down_hbm, tiles_d, load_sem.at[2]),
        pltpu.make_async_copy(ga_hbm, ab.at[pl.ds(0, rank), :], load_sem.at[3]),
        pltpu.make_async_copy(ua_hbm, ab.at[pl.ds(rank, rank), :], load_sem.at[4]),
        pltpu.make_async_copy(db_hbm, wd.at[pl.ds(hidden, rank), :], load_sem.at[5]),
    ]
    for load in loads:
        load.start()

    xin = x_ref[...].astype(F32)
    scale_rms = lax.rsqrt(jnp.mean(xin * xin, axis=1, keepdims=True) + EPSILON)
    normed = xin * scale_rms
    given = go_ref[...].astype(F32)
    for k in range(nx):
        a2a_send[k, :, 0:slab] = normed[:, k * slab : (k + 1) * slab]
        a2a_send[k, :, slab : 2 * slab] = given[:, k * slab : (k + 1) * slab]
        a2a_send[k, :, 2 * slab : 2 * slab + TILE] = jnp.broadcast_to(scale_rms, (rows_q, TILE))

    pl.semaphore_wait(barrier, (nx - 1) + (nz - 1) + 1 + 2 * nz)

    def a2a(i):
        return remote(
            a2a_send.at[lax.rem(x + i + 1, nx)],
            a2a_recv.at[x],
            a2a_ss.at[i],
            a2a_rs.at[i],
            tensor=x_peer(i + 1),
        )

    each(nx - 1, lambda i: a2a(i).start())
    a2a_recv[x] = a2a_send[x]
    each(nx - 1, lambda i: a2a(i).wait())
    for k in range(nx):
        n16[k * rows_q : (k + 1) * rows_q, :] = a2a_recv[k, :, 0:slab]
        dx32[k * rows_q : (k + 1) * rows_q, :] = a2a_recv[k, :, slab : 2 * slab]
        r16[k * rows_q : (k + 1) * rows_q, :] = a2a_recv[k, :, 2 * slab : 2 * slab + TILE]
    gain = gain_ref[:, aligned(x, slab)].astype(F32)
    mine = aligned(z, zt)
    u_all[x, mine, :] = (n16[...] * gain).astype(BF16)

    def cols(h):
        return pl.ds(h * half, half)

    def u_z(h, i):
        place = u_all.at[x, mine, cols(h)]
        return remote(
            place, place, uz_ss.at[h * nz + i], uz_rs.at[h * nz + z], tensor=z_peer(i + 1)
        )

    def given_z(h, i):
        place = g_all.at[x, mine, cols(h)]
        return remote(
            place, place, gz_ss.at[h * nz + i], gz_rs.at[h * nz + z], tensor=z_peer(i + 1)
        )

    def sent_z(h, i):
        return remote(
            dx16.at[:, cols(h)],
            g_all.at[x, mine, cols(h)],
            gz_ss.at[h * nz + i],
            gz_rs.at[h * nz + z],
            pipe=below,
            tensor=z_peer(i),
        )

    def came_z(buf, rs, h, source):
        place = buf.at[x, aligned(source, zt), cols(h)]
        remote(place, place, rs.at[h * nz + source], rs.at[h * nz + source], pipe=above).wait_recv()

    def direct(buf, ss, rs, side, h):
        place = buf.at[x, :, cols(h)]
        return remote(
            place, place, ss.at[side * 2 + h], rs.at[side * 2 + h], tensor=side_peer(side)
        )

    def relay(buf, ss, rs, side, h):
        place = buf.at[left if side == 0 else right, :, pl.ds((2 * h + side) * quarter, quarter)]
        return remote(
            place, place, ss.at[side * 2 + h], rs.at[side * 2 + h], tensor=side_peer(side)
        )

    def send_direct(buf, ss, rs, wait_z):
        for h in range(2):
            wait_z(h)
            for side in range(2):
                direct(buf, ss, rs, side, h).start()

    def send_relays(buf, dss, drs, rss, rrs):
        for h in range(2):
            for side in range(2):
                direct(buf, dss, drs, side, h).wait_recv()
                relay(buf, rss, rrs, side, h).start()

    for h in range(2):
        each(nz - 1, lambda i: u_z(h, i).start())

    @pl.when(last)
    def _():
        g_all[x, mine, :] = dx32[...].astype(BF16)
        for h in range(2):
            each(nz - 1, lambda i: given_z(h, i).start())

    gub[...] = jnp.zeros_like(gub)
    dax[...] = jnp.zeros_like(dax)
    gub[0:rank, 0:hidden] = gb_ref[...]
    gub[rank : 2 * rank, hidden : 2 * hidden] = ub_ref[...]
    dax[0:rank, :] = da_ref[...]
    wd[hidden + rank : hidden + TILE, :] = jnp.zeros((TILE - rank, width), BF16)

    def placed(tiles, member, block):
        slot = inv[member, block]
        tile = tiles[jnp.maximum(slot, 0)]
        return jnp.where(slot >= 0, tile, jnp.zeros_like(tile))

    loads[0].wait()

    def build_gate(r):
        for c in range(col_blocks):
            wgu[aligned(r, TILE), c * TILE : (c + 1) * TILE] = placed(tiles_g, 0, r * col_blocks + c)

    each(row_blocks, build_gate)

    def own_u_z(h):
        each(nz - 1, lambda i: came_z(u_all, uz_rs, h, lax.rem(z + i + 1, nz)))

    send_direct(u_all, ud_ss, ud_rs, own_u_z)

    loads[1].wait()

    def build_up(r):
        for c in range(col_blocks):
            wgu[aligned(r, TILE), hidden + c * TILE : hidden + (c + 1) * TILE] = placed(
                tiles_u, 1, r * col_blocks + c
            )

    each(row_blocks, build_up)
    send_relays(u_all, ud_ss, ud_rs, ur_ss, ur_rs)
    loads[2].wait()

    def build_down(c):
        for r in range(col_blocks):
            wd[r * TILE : (r + 1) * TILE, aligned(c, TILE)] = placed(tiles_d, 2, r * row_blocks + c)

    each(row_blocks, build_down)
    for load in loads[3:]:
        load.wait()

    def given_came(h):
        each(nz - 1, lambda i: came_z(g_all, gz_rs, h, lax.rem(z + i + 1, nz)))

    def sent_came(h):
        each(nz, lambda i: came_z(g_all, gz_rs, h, i))

    @pl.when(last)
    def _():
        send_direct(g_all, gd_ss, gd_rs, given_came)

    acc_gu[...] = jnp.zeros_like(acc_gu)
    acc_a[...] = jnp.zeros_like(acc_a)

    def forward(i):
        k = lax.rem(x + jnp.where(i == 2, 3, jnp.where(i == 3, 2, i)), nx)

        @pl.when(i == 3)
        def _():
            for h in range(2):
                for side in range(2):
                    relay(u_all, ur_ss, ur_rs, side, h).wait_recv()

        acc_gu[...] += dot_nn(u_all[k], wgu[aligned(k, slab), :])
        acc_a[...] += dot_nt(u_all[k], ab[:, aligned(k, slab)])

    each(nx, forward)
    a_gu[...] = acc_a[...].astype(BF16)
    acc_gu[...] += SCALE * dot_nn(a_gu[...], gub[...])

    @pl.when(jnp.logical_not(last))
    def _():
        send_direct(g_all, gd_ss, gd_rs, sent_came)

    acc_d[...] = jnp.zeros_like(acc_d)

    def hidden_grad(i):
        k = lax.rem(x + jnp.where(i == 2, 3, jnp.where(i == 3, 2, i)), nx)

        @pl.when(i == 1)
        def _():
            send_relays(g_all, gd_ss, gd_rs, gr_ss, gr_rs)

        @pl.when(i == 3)
        def _():
            for h in range(2):
                for side in range(2):
                    relay(g_all, gr_ss, gr_rs, side, h).wait_recv()

        acc_d[...] += dot_nt(g_all[k], wd[:, aligned(k, slab)])

    each(nx, hidden_grad)
    c_lr[...] = acc_d[:, hidden : hidden + TILE].astype(BF16)
    acc_d[:, 0:hidden] += SCALE * dot_nn(c_lr[...], dax[...])

    lane = lax.broadcasted_iota(jnp.int32, (zt, TILE), 1)
    row = lax.broadcasted_iota(jnp.int32, (zt, TILE), 0)
    m_send[...] = jnp.zeros_like(m_send)

    def middle(j):
        rows = aligned(j, zt)
        gate = acc_gu[rows, 0:hidden]
        up = acc_gu[rows, hidden : 2 * hidden]
        dh = acc_d[rows, 0:hidden]
        q = jax.nn.sigmoid(gate)
        active = gate * q
        hid[rows, :] = (active * up).astype(BF16)
        dgate = (dh * up * (q * (1.0 + gate * (1.0 - q)))).astype(BF16)
        dup = (dh * active).astype(BF16)
        dgu[rows, 0:hidden] = dgate
        dgu[rows, hidden : 2 * hidden] = dup
        dots = jnp.sum(dgate.astype(F32) * gate + dup.astype(F32) * up, axis=1, keepdims=True)
        spread = jnp.sum(jnp.where(lane == row + j * zt, dots, 0.0), axis=0, keepdims=True)
        m_send[...] += jnp.broadcast_to(spread, m_send.shape)

    each(nz, middle)

    def m_copy(i):
        return remote(m_send, m_recv.at[i], m_ss.at[i], m_rs.at[i], tensor=x_peer(i + 1))

    each(nx - 1, lambda i: m_copy(i).start())
    tm[:, 0:TILE] = dot_nt(dgu[...], gub[...])
    ta[...] = (SCALE * tm[:, 0:TILE]).astype(BF16)

    def partial(k):
        return dot_nt(dgu[...], wgu[aligned(k, slab), :]) + dot_nn(ta[...], ab[:, aligned(k, slab)])

    def part(q):
        return pl.ds(q * quarter, quarter)

    def far(side, h):
        return remote(
            s_far.at[:, part(2 * h + side)],
            r_far.at[side, h],
            far_ss.at[side * 2 + h],
            far_rs.at[side * 2 + h],
            tensor=side_peer(side),
        )

    def near(side, q):
        return remote(
            s_near.at[side, :, part(q)],
            r_near.at[side, :, part(q)],
            near_ss.at[side * 4 + q],
            near_rs.at[side * 4 + q],
            tensor=side_peer(side),
        )

    s_far[...] = partial(across).astype(BF16)
    for h in range(2):
        for side in range(2):
            far(side, h).start()

    s_near[0] = partial(right).astype(BF16)
    near(0, 1).start()
    s_near[1] = partial(left).astype(BF16)
    near(1, 0).start()
    total[...] = partial(x)

    for h in range(2):
        for side in range(2):
            q = 2 * h + side
            far(side, h).wait_recv()
            s_near[side, :, part(q)] = (
                s_near[side, :, part(q)].astype(F32) + r_far[side, h].astype(F32)
            ).astype(BF16)
            near(side, q).start()
        if h == 0:
            near(0, 3).start()
            near(1, 2).start()

    tm[:, TILE : 2 * TILE] = dot_nt(hid[...], dax[...])
    t_send[...] = tm[...].astype(BF16)
    grads = SCALE * dot_tn(a_gu[...], dgu[...])
    hid_own[0:rank, :] = grads[0:rank, 0:hidden].astype(BF16)
    hid_own[rank : 2 * rank, :] = grads[rank : 2 * rank, hidden : 2 * hidden].astype(BF16)
    hid_own[2 * rank : 3 * rank, :] = (SCALE * dot_tn(c_lr[...], hid[...]))[0:rank, :].astype(BF16)

    def swap(src, dst, i):
        return remote(src, dst, dp_ss.at[i], dp_rs.at[i], dp=1 - core)

    swap(hid_own, hid_recv, 0).start()

    def z_lanes(h):
        return pl.ds(0, TILE + half) if h == 0 else pl.ds(TILE + half, half)

    def z_copy(h, i):
        return remote(
            z_send.at[aligned(lax.rem(z + i + 1, nz), zt), z_lanes(h)],
            z_recv.at[i, :, z_lanes(h)],
            rz_ss.at[h * nz + i],
            rz_rs.at[h * nz + i],
            tensor=z_peer(i + 1),
        )

    each(nx - 1, lambda i: m_copy(i).wait())
    dots_row = m_send[...]
    for i in range(nx - 1):
        dots_row = dots_row + m_recv[i]
    m_send[...] = dots_row

    for h in range(2):
        for q in (2 * h, 2 * h + 1):
            for side in range(2):
                near(side, q).wait_recv()

        def add_slabs(j):
            rows = aligned(j, zt)
            value = (
                total[rows, cols(h)]
                + r_near[0, rows, cols(h)].astype(F32)
                + r_near[1, rows, cols(h)].astype(F32)
            )
            total[rows, cols(h)] = value
            z_send[rows, pl.ds(TILE + h * half, half)] = value.astype(BF16)
            if h == 0:
                column = jnp.sum(
                    jnp.where(lane == row + j * zt, m_send[0:1, :], 0.0), axis=1, keepdims=True
                )
                z_send[rows, 0:TILE] = jnp.broadcast_to(column, (zt, TILE)).astype(BF16)

        each(nz, add_slabs)
        each(nz - 1, lambda i: z_copy(h, i).start())

    def t_x(i):
        return remote(t_send, t_recv.at[i], tx_ss.at[i], tx_rs.at[i], tensor=x_peer(i + 1))

    each(nx - 1, lambda i: t_x(i).start())

    row_scale = r16[:, 0:1]
    mean = None
    for h in range(2):
        each(nz - 1, lambda i: z_copy(h, i).wait_recv())
        if h == 0:
            mean = z_send[mine, 0:TILE].astype(F32)
            for i in range(nz - 1):
                mean = mean + z_recv[i, :, 0:TILE].astype(F32)
            mean = mean[:, 0:1] / width
        value = total[mine, cols(h)]
        for i in range(nz - 1):
            value = value + z_recv[i, :, pl.ds(TILE + h * half, half)].astype(F32)
        dn = value * gain[:, h * half : (h + 1) * half]
        dx = g_all[x, mine, cols(h)].astype(F32) + row_scale * (dn - n16[:, cols(h)] * mean)
        dx16[:, cols(h)] = dx.astype(BF16)

        @pl.when(pipe > 0)
        def _():
            each(nz, lambda i: sent_z(h, i).start())

    each(nx - 1, lambda i: t_x(i).wait())
    t_sum = tm[...]
    for i in range(nx - 1):
        t_sum = t_sum + t_recv[i].astype(F32)
    tm[...] = t_sum
    tz_send[...] = t_sum.astype(BF16)

    def t_reduce(i):
        return remote(
            tz_send.at[aligned(lax.rem(z + i + 1, nz), zt)],
            tz_recv.at[i],
            tr_ss.at[i],
            tr_rs.at[i],
            tensor=z_peer(i + 1),
        )

    each(nz - 1, lambda i: t_reduce(i).start())

    dx32[...] = dx16[...].astype(F32)
    for k in range(nx):
        o_send[k] = dx32[k * rows_q : (k + 1) * rows_q, :]

    def o_copy(i):
        return remote(
            o_send.at[lax.rem(x + i + 1, nx)],
            o_recv.at[x],
            o_ss.at[i],
            o_rs.at[i],
            tensor=x_peer(i + 1),
        )

    each(nx - 1, lambda i: o_copy(i).start())
    o_recv[x] = o_send[x]

    each(nz - 1, lambda i: t_reduce(i).wait())
    t_mine = tm[mine, :]
    for i in range(nz - 1):
        t_mine = t_mine + tz_recv[i].astype(F32)
    t_all[mine, :] = t_mine.astype(BF16)

    def t_gather(i):
        return remote(
            t_all.at[mine], t_all.at[mine], ta_ss.at[i], ta_rs.at[i], tensor=z_peer(i + 1)
        )

    each(nz - 1, lambda i: t_gather(i).start())

    each(nx - 1, lambda i: o_copy(i).wait())
    for k in range(nx):
        dx_out[:, k * slab : (k + 1) * slab] = o_recv[k].astype(BF16)

    each(nz - 1, lambda i: t_gather(i).wait())

    def wide(k):
        columns = aligned(k, slab)
        wide_own[0 : 2 * rank, columns] = (
            SCALE * dot_tn(t_all[:, 0:TILE], u_all[k])
        ).astype(BF16)
        wide_own[2 * rank : 3 * rank, columns] = (
            SCALE * dot_tn(t_all[:, TILE : 2 * TILE], g_all[k])
        )[0:rank, :].astype(BF16)

    each(nx, wide)
    swap(wide_own, wide_recv, 1).start()

    for h in range(2):
        each(nz - 1, lambda i: u_z(h, i).wait_send())
        each(nz - 1, lambda i: z_copy(h, i).wait_send())
        for side in range(2):
            direct(u_all, ud_ss, ud_rs, side, h).wait_send()
            relay(u_all, ur_ss, ur_rs, side, h).wait_send()
            direct(g_all, gd_ss, gd_rs, side, h).wait_send()
            relay(g_all, gr_ss, gr_rs, side, h).wait_send()
            far(side, h).wait_send()
    for q in range(4):
        for side in range(2):
            near(side, q).wait_send()

    @pl.when(last)
    def _():
        for h in range(2):
            each(nz - 1, lambda i: given_z(h, i).wait_send())

    @pl.when(pipe > 0)
    def _():
        for h in range(2):
            each(nz, lambda i: sent_z(h, i).wait_send())

    swap(hid_own, hid_recv, 0).wait()
    swap(wide_own, wide_recv, 1).wait()


def finish_kernel(
    dx, wide_own, wide_recv, hid_own, hid_recv, dx_out, ga_out, ua_out, db_out, gb_out, ub_out, da_out
):
    rank = ga_out.shape[0]
    dx_out[...] = dx[...]
    for index, out in enumerate((ga_out, ua_out, db_out)):
        rows = slice(index * rank, (index + 1) * rank)
        out[...] = (wide_own[rows, :].astype(F32) + wide_recv[rows, :].astype(F32)).astype(BF16)
    for index, out in enumerate((gb_out, ub_out, da_out)):
        rows = slice(index * rank, (index + 1) * rank)
        out[...] = (hid_own[rows, :].astype(F32) + hid_recv[rows, :].astype(F32)).astype(BF16)


def shards(
    states,
    out_grad,
    norm_gain,
    gate_tiles,
    up_tiles,
    down_tiles,
    tile_lists,
    tile_counts,
    gate_a,
    gate_adapter_output,
    up_a,
    upper_adapter_output,
    down_adapter_input,
    down_b,
):
    pipe_n = lax.axis_size("pipe")
    tensor_n = lax.axis_size("tensor")
    nx = X_CHIPS
    nz = tensor_n // nx
    rows_q, width = states.shape[2:]
    slots = gate_tiles.shape[1]
    rank = gate_a.shape[2]
    hidden = gate_adapter_output.shape[2]
    tokens = rows_q * tensor_n
    zt = rows_q * nx
    slab = width // nx
    row_blocks, col_blocks = width // TILE, hidden // TILE
    blocks = row_blocks * col_blocks

    places = tile_lists[0]
    strides = jnp.array([col_blocks, col_blocks, row_blocks], jnp.int32)[:, None]
    place = places[:, :, 0] * strides + places[:, :, 1]
    slot_ids = jnp.arange(slots, dtype=jnp.int32)
    alive = slot_ids[None, :] < tile_counts[0]
    hit = jnp.logical_and(
        place[:, None, :] == jnp.arange(blocks, dtype=jnp.int32)[None, :, None], alive[:, None, :]
    )
    inv = jnp.max(jnp.where(hit, slot_ids[None, None, :], -1), axis=2)

    vmem = pl.BlockSpec(memory_space=pltpu.VMEM)
    anywhere = pl.BlockSpec(memory_space=pl.ANY)
    smem = pl.BlockSpec(memory_space=pltpu.SMEM)
    dma = pltpu.SemaphoreType.DMA
    vm = pltpu.VMEM
    scratch = [
        vm((slots, TILE, TILE), BF16),
        vm((slots, TILE, TILE), BF16),
        vm((slots, TILE, TILE), BF16),
        vm((width, 2 * hidden), BF16),
        vm((hidden + TILE, width), BF16),
        vm((TILE, width), BF16),
        vm((TILE, 2 * hidden), BF16),
        vm((TILE, hidden), BF16),
        vm((nx, rows_q, 2 * slab + TILE), F32),
        vm((nx, rows_q, 2 * slab + TILE), F32),
        vm((zt, slab), F32),
        vm((zt, TILE), F32),
        vm((zt, slab), F32),
        vm((zt, slab), BF16),
        vm((nx, tokens, slab), BF16),
        vm((nx, tokens, slab), BF16),
        vm((tokens, 2 * hidden), F32),
        vm((tokens, TILE), F32),
        vm((tokens, hidden + TILE), F32),
        vm((tokens, TILE), BF16),
        vm((tokens, TILE), BF16),
        vm((tokens, hidden), BF16),
        vm((tokens, 2 * hidden), BF16),
        vm((tokens, TILE), BF16),
        vm((tokens, EXTRA), F32),
        vm((8, TILE), F32),
        vm((nx - 1, 8, TILE), F32),
        vm((tokens, slab), BF16),
        vm((2, 2, tokens, slab // 4), BF16),
        vm((2, tokens, slab), BF16),
        vm((2, tokens, slab), BF16),
        vm((tokens, slab), F32),
        vm((tokens, TILE + slab), BF16),
        vm((nz - 1, zt, TILE + slab), BF16),
        vm((nx, rows_q, slab), F32),
        vm((nx, rows_q, slab), F32),
        vm((tokens, EXTRA), BF16),
        vm((nx - 1, tokens, EXTRA), BF16),
        vm((tokens, EXTRA), BF16),
        vm((nz - 1, zt, EXTRA), BF16),
        vm((tokens, EXTRA), BF16),
        dma((6,)),
    ]
    x_n, z_n, z_2 = nx - 1, nz - 1, 2 * nz
    for count in (x_n, z_2, 4, 4, z_2, 4, 4, x_n, 4, 8, z_2, x_n, x_n, z_n, z_n, 2):
        scratch += [dma((count,)), dma((count,))]
    dx, wide_own, wide_recv, hid_own, hid_recv = pl.pallas_call(
        functools.partial(section_kernel, (pipe_n, nz, nx, hidden, width)),
        out_shape=(
            jax.ShapeDtypeStruct((rows_q, width), BF16),
            jax.ShapeDtypeStruct((3 * rank, width), BF16),
            jax.ShapeDtypeStruct((3 * rank, width), BF16),
            jax.ShapeDtypeStruct((3 * rank, hidden), BF16),
            jax.ShapeDtypeStruct((3 * rank, hidden), BF16),
        ),
        in_specs=[smem, vmem, vmem, vmem] + [anywhere] * 6 + [vmem] * 3,
        out_specs=[vmem] * 5,
        scratch_shapes=scratch,
        compiler_params=pltpu.CompilerParams(
            collective_id=0, has_side_effects=True, vmem_limit_bytes=56 * 1024 * 1024
        ),
        cost_estimate=pl.CostEstimate(
            flops=10 * tokens * width * hidden,
            bytes_accessed=6 * slots * TILE * TILE,
            transcendentals=tokens * hidden,
        ),
    )(
        inv,
        states[0, 0],
        out_grad[0],
        norm_gain,
        gate_tiles[0],
        up_tiles[0],
        down_tiles[0],
        gate_a[0].T,
        up_a[0].T,
        down_b[0],
        gate_adapter_output[0],
        upper_adapter_output[0],
        down_adapter_input[0].T,
    )
    full = jax.ShapeDtypeStruct((rank, width), BF16)
    part = jax.ShapeDtypeStruct((rank, hidden), BF16)
    dx, ga, ua, db, gb, ub, da = pl.pallas_call(
        finish_kernel,
        out_shape=(jax.ShapeDtypeStruct((rows_q, width), BF16), full, full, full, part, part, part),
        in_specs=[vmem] * 5,
        out_specs=[vmem] * 7,
    )(dx, wide_own, wide_recv, hid_own, hid_recv)
    return dx[None, None], ga.T[None], gb[None], ua.T[None], ub[None], da.T[None], db[None]


def solution(mesh):
    placed = (
        P("pipe", "dp", "tensor", None),
        P("dp", "tensor", None),
        P("pipe", None),
        P("pipe", "tensor", None, None),
        P("pipe", "tensor", None, None),
        P("pipe", "tensor", None, None),
        P("pipe", None, "tensor", None),
        P("pipe", None, "tensor"),
        P("pipe", None, None),
        P("pipe", None, "tensor"),
        P("pipe", None, None),
        P("pipe", None, "tensor"),
        P("pipe", "tensor", None),
        P("pipe", None, None),
    )
    return jax.shard_map(
        shards,
        mesh=mesh,
        in_specs=placed,
        out_specs=(
            P("pipe", "dp", "tensor", None),
            P("pipe", None, None),
            P("pipe", None, "tensor"),
            P("pipe", None, None),
            P("pipe", None, "tensor"),
            P("pipe", "tensor", None),
            P("pipe", None, None),
        ),
        check_vma=False,
    )
```

time: 256 us -> 204 us (0.80)
  Pallas kernels: 237 us -> 200 us
  local copies, waits for them, and re-layouts: 14.5 us -> 0.76 us
    pallas_call x1, Pallas kernels: 237 us -> 197 us  [shards(): pl.pallas_call(functools.partial(section_kernel, (pipe_n, nz, nx, hidden,...]
    unnamed x12 -> x0, local copies, waits for them, and re-layouts: 9.15 us -> none
    broadcast_in_dim x3 -> x0, local copies, waits for them, and re-layouts: 4.58 us -> none  [the longest x1 2.05 us: shards(): ab_grad[None, :, rank:]]
    pallas_call x0 -> x1, Pallas kernels: none -> 3.32 us  [shards(): pl.pallas_call(finish_kernel, out_shape=(jax.ShapeDtypeStruct((rows_q, wi...]
where the time goes in v2:
time: 204 us
  Pallas kernels  200 us (98%)
  other arithmetic  2.23 us (1%)
    pallas_call x1, Pallas kernels, shards(): pl.pallas_call(functools.partial(section_kernel, (pipe_n, nz, nx, hidden,...  197 us

profile of v2, /device:TPU:1, one launch (start us, length us, event | category | flops | bytes accessed | tf_op | source)
XLA Modules:
  0.0 203.9 jit_solution(11286780266868570556)
XLA Ops:
  0.6 0.7 iota_compare_fusion.1
  1.4 0.8 fusion.3
  2.1 0.7 fusion.2
  2.8 0.8 select_reduce_fusion.inv
  3.6 196.9 %shard_map.198 = (bf16[4,4096]{1,0:T(4,128)(2,1)}, bf16[192,4096]{1,0:T(8,128)(2,1)}, bf16[192,4096]{1,0:T(8,128)(2,1)}, bf16[192,640]{1,0:T(8,128)(2,1)}, bf16[192,640]{1,0:T(8,128)(2,1)}) custom-call(s32[3,160]{1,0:T(4,128)} %select_reduce_fusion.inv, bf16[4,4096]{1,0:T(4,128)(2,1)} %bitcast.49, bf16[4,4096]{1,0:T(4,128)(2,1)} %bitcast.50, ...), custom_call_target="tpu_custom_call" | custom-call | flops 3355443200 | bytes 10813440 | tf_op jit(solution)/shard_map/pallas_call | solution.py:739
  200.5 3.3 %shard_map.199 = (bf16[4,4096]{1,0:T(4,128)(2,1)}, bf16[64,4096]{1,0:T(8,128)(2,1)}, bf16[64,4096]{1,0:T(8,128)(2,1)}, bf16[64,4096]{1,0:T(8,128)(2,1)}, bf16[64...) custom-call(bf16[4,4096]{1,0:T(4,128)(2,1)} %get-tuple-element.19.dx, ...), custom_call_target="tpu_custom_call" | custom-call | tf_op jit(solution)/shard_map/pallas_call | solution.py:776
